TPU v7x, 512 devices: a whole 4x4x16 slice. The times are simulated.
512 devices in a mesh: head: 16 (over y, x), seq: 32 (over z, core).
Axes of the slice: x: 4, y: 4, z: 16, core: 2. Of those that a mesh axis runs over, the one named last changes fastest.
Arguments:
- queries: bfloat16 [65536, 2048], P(('seq', 'head')), may hold values from -6 to 6
- key_vectors: bfloat16 [65536, 2048], P(('seq', 'head')), may hold values from -6 to 6
- value_vectors: bfloat16 [65536, 2048], P(('seq', 'head')), may hold values from -6 to 6
- cotangent: bfloat16 [65536, 2048], P(('seq', 'head')), may hold values from -6 to 6
Outputs:
- normed_out: bfloat16 [65536, 2048], P(('seq', 'head'))
- query_grad: bfloat16 [65536, 2048], P(('seq', 'head'))
- key_grad: bfloat16 [65536, 2048], P(('seq', 'head'))
- value_grad: bfloat16 [65536, 2048], P(('seq', 'head'))
All inputs are finite; a program needn't handle non-finite values.
Results may differ from a plain program's by a relative error of at most 0.005.
Values may be sent and summed in bfloat16 or wider, within the bound.
A program may use at most 64 MiB of HBM per device.

v0:
```python
import jax
import jax.numpy as jnp
from jax import lax
from jax.sharding import PartitionSpec as P

DH = 128


epsilon = 1e-06


def shards(queries, key_vectors, value_vectors, cotangent):
    query_heads, key_heads, value_heads, cot_heads = (
        lax.all_to_all(queries, "head", split_axis=1, concat_axis=0, tiled=True),
        lax.all_to_all(key_vectors, "head", split_axis=1, concat_axis=0, tiled=True),
        lax.all_to_all(value_vectors, "head", split_axis=1, concat_axis=0, tiled=True),
        lax.all_to_all(cotangent, "head", split_axis=1, concat_axis=0, tiled=True),
    )
    tokens_here = query_heads.shape[0]
    block_len = tokens_here // 2
    head_size = DH
    heads_here = query_heads.shape[1] // head_size
    width = heads_here * head_size
    query_heads = query_heads.reshape(2, block_len, heads_here, head_size)
    key_heads = key_heads.reshape(2, block_len, heads_here, head_size)
    value_heads = value_heads.reshape(2, block_len, heads_here, head_size)
    cot_heads = cot_heads.reshape(2, block_len, heads_here, head_size)
    my_slab = lax.axis_index("seq")
    slab_kv = jnp.einsum(
        "blhd,blhe->bhde", key_heads, value_heads, preferred_element_type=jnp.float32
    )
    device_kv = slab_kv[0] + slab_kv[1]
    shard_block = lax.all_gather(device_kv[None], "seq", axis=0, tiled=True)
    indices = jnp.arange(shard_block.shape[0], dtype=jnp.int32)
    earlier = (indices < my_slab).astype(jnp.float32)
    prefix = jnp.sum(earlier[:, None, None, None] * shard_block, axis=0)
    state_pair = jnp.stack([prefix, prefix + slab_kv[0]])
    positions = jnp.arange(block_len, dtype=jnp.int32)
    causal = positions[:, None] >= positions[None, :]
    scores = jnp.einsum(
        "blhd,bmhd->bhlm", query_heads, key_heads, preferred_element_type=jnp.float32
    )
    masked_scores = jnp.where(causal[None, None], scores, jnp.float32(0.0)).astype(jnp.bfloat16)
    attn_out = jnp.einsum(
        "bhlm,bmhd->blhd", masked_scores, value_heads, preferred_element_type=jnp.float32
    )
    attn_out = attn_out + jnp.einsum(
        "blhd,bhde->blhe",
        query_heads.astype(jnp.float32),
        state_pair,
        precision=lax.Precision.HIGHEST,
    )
    inv_rms = lax.rsqrt(jnp.mean(attn_out * attn_out, axis=-1, keepdims=True) + epsilon)
    normed = attn_out * inv_rms
    normed_bf = normed.astype(jnp.bfloat16).reshape(tokens_here, width)
    normed_out = lax.all_to_all(normed_bf, "head", split_axis=0, concat_axis=1, tiled=True)
    cot_float = cot_heads.astype(jnp.float32)
    out_grad = (
        inv_rms * (cot_float - normed * jnp.mean(cot_float * normed, axis=-1, keepdims=True))
    ).astype(jnp.bfloat16)
    slab_grad = jnp.einsum(
        "blhd,blhe->bhde", query_heads, out_grad, preferred_element_type=jnp.float32
    )
    device_grad = slab_grad[0] + slab_grad[1]
    shard_block = lax.all_gather(device_grad[None], "seq", axis=0, tiled=True)
    indices = jnp.arange(shard_block.shape[0], dtype=jnp.int32)
    later = (indices > my_slab).astype(jnp.float32)
    suffix = jnp.sum(later[:, None, None, None] * shard_block, axis=0)
    grad_pair = jnp.stack([suffix + slab_grad[1], suffix])
    grads = jnp.einsum("blhe,bmhe->bhlm", out_grad, value_heads, preferred_element_type=jnp.float32)
    masked_grads = jnp.where(causal[None, None], grads, jnp.float32(0.0)).astype(jnp.bfloat16)
    query_grad = jnp.einsum(
        "bhlm,bmhd->blhd", masked_grads, key_heads, preferred_element_type=jnp.float32
    )
    query_grad = query_grad + jnp.einsum(
        "blhe,bhde->blhd", out_grad.astype(jnp.float32), state_pair, precision=lax.Precision.HIGHEST
    )
    key_grad = jnp.einsum(
        "bhlm,blhd->bmhd", masked_grads, query_heads, preferred_element_type=jnp.float32
    )
    key_grad = key_grad + jnp.einsum(
        "bmhe,bhde->bmhd",
        value_heads.astype(jnp.float32),
        grad_pair,
        precision=lax.Precision.HIGHEST,
    )
    value_grad = jnp.einsum(
        "bhlm,blhe->bmhe", masked_scores, out_grad, preferred_element_type=jnp.float32
    )
    value_grad = value_grad + jnp.einsum(
        "bmhd,bhde->bmhe", key_heads.astype(jnp.float32), grad_pair, precision=lax.Precision.HIGHEST
    )
    query_bf = query_grad.astype(jnp.bfloat16).reshape(tokens_here, width)
    key_bf = key_grad.astype(jnp.bfloat16).reshape(tokens_here, width)
    value_bf = value_grad.astype(jnp.bfloat16).reshape(tokens_here, width)
    query_back, key_back, value_back = (
        lax.all_to_all(query_bf, "head", split_axis=0, concat_axis=1, tiled=True),
        lax.all_to_all(key_bf, "head", split_axis=0, concat_axis=1, tiled=True),
        lax.all_to_all(value_bf, "head", split_axis=0, concat_axis=1, tiled=True),
    )
    return (normed_out, query_back, key_back, value_back)


def solution(mesh):
    return jax.shard_map(
        shards,
        mesh=mesh,
        in_specs=(
            P(("seq", "head"), None),
            P(("seq", "head"), None),
            P(("seq", "head"), None),
            P(("seq", "head"), None),
        ),
        out_specs=(
            P(("seq", "head"), None),
            P(("seq", "head"), None),
            P(("seq", "head"), None),
            P(("seq", "head"), None),
        ),
        check_vma=False,
    )
```

profile of v0, /device:TPU:1, one launch (start us, length us, event | category | flops | bytes accessed | tf_op | source)
XLA Modules:
  0.0 234.3 jit_solution(17913855510241784192)
XLA Ops:
  7.2 0.0 copy-start
  7.2 1.0 copy-done
  8.2 0.9 copy_bitcast_fusion.5
  9.1 7.6 %all-to-all-start.1 = ((bf16[128,16,128]{2,0,1:T(8,128)(2,1)}), bf16[128,16,128]{2,0,1:T(8,128)(2,1)S(1)}, u32[]{:S(2)}, u32[]{:S(2)}) async-start(bf16[128,16,128]{2,0,1:T(8,128)(2,1)} %copy_bitcast_fusion.5), calls=%async_computation.1 | async-start | bytes 1048576 | tf_op jit(solution)/shard_map/all_to_all | solution.py:15
  16.7 0.0 all-gather.5.cloned.1.call-start
  16.8 1.2 copy_bitcast_fusion.4
  18.0 7.8 %all-to-all-done.1 = bf16[128,16,128]{2,0,1:T(8,128)(2,1)S(1)} async-done(((bf16[128,16,128]{2,0,1:T(8,128)(2,1)}), bf16[128,16,128]{2,0,1:T(8,128)(2,1)S(1)}, u32[]{:S(2)}, u32[]{:S(2)}) %all-to-all-start.1) | async-done | bytes 524320 | tf_op jit(solution)/shard_map/all_to_all | solution.py:15
  25.7 11.7 %all_to_all.137 = bf16[128,16,128]{2,0,1:T(8,128)(2,1)S(1)} all-to-all(bf16[128,16,128]{2,0,1:T(8,128)(2,1)S(1)} %copy_bitcast_fusion.4), channel_id=1, replica_groups=mesh['head'=16,'seq'=32] {'head'}, dimensions={1} | all-to-all | bytes 1048576 | tf_op jit(solution)/shard_map/all_to_all | solution.py:16
  37.5 0.3 fusion.18
  37.8 0.6 slice_add_fusion.1
  38.5 0.0 all-gather.5.cloned.1.call-update
  38.5 0.9 copy_bitcast_fusion.3
  39.4 3.6 %all-to-all-start.4 = ((bf16[128,16,128]{2,0,1:T(8,128)(2,1)}), bf16[128,16,128]{2,0,1:T(8,128)(2,1)S(1)}, u32[]{:S(2)}, u32[]{:S(2)}) async-start(bf16[128,16,128]{2,0,1:T(8,128)(2,1)} %copy_bitcast_fusion.3), calls=%async_computation.4 | async-start | bytes 1048576 | tf_op jit(solution)/shard_map/all_to_all | solution.py:17
  43.0 0.0 copy-done.15
  43.0 0.9 copy_bitcast_fusion.6
  43.9 8.0 %all-to-all-done.4 = bf16[128,16,128]{2,0,1:T(8,128)(2,1)S(1)} async-done(((bf16[128,16,128]{2,0,1:T(8,128)(2,1)}), bf16[128,16,128]{2,0,1:T(8,128)(2,1)S(1)}, u32[]{:S(2)}, u32[]{:S(2)}) %all-to-all-start.4) | async-done | bytes 524320 | tf_op jit(solution)/shard_map/all_to_all | solution.py:17
  52.0 0.8 copy-done.11
  52.8 3.6 %all-to-all-start = ((bf16[128,16,128]{2,0,1:T(8,128)(2,1)}), bf16[128,16,128]{2,0,1:T(8,128)(2,1)S(1)}, u32[]{:S(2)}, u32[]{:S(2)}) async-start(bf16[128,16,128]{2,0,1:T(8,128)(2,1)} %copy_bitcast_fusion.6), calls=%async_computation | async-start | bytes 1048576 | tf_op jit(solution)/shard_map/all_to_all | solution.py:14
  56.3 0.0 all-gather.7.cloned.1.call-start
  56.4 1.3 iota_compare_fusion
  57.7 1.1 convert_element_type.95
  58.8 6.5 %all-to-all-done = bf16[128,16,128]{2,0,1:T(8,128)(2,1)S(1)} async-done(((bf16[128,16,128]{2,0,1:T(8,128)(2,1)}), bf16[128,16,128]{2,0,1:T(8,128)(2,1)S(1)}, u32[]{:S(2)}, u32[]{:S(2)}) %all-to-all-start) | async-done | bytes 524320 | tf_op jit(solution)/shard_map/all_to_all | solution.py:14
  65.3 2.9 %select_convert_fusion.1 = bf16[2,1024,1024]{2,1,0:T(8,128)(2,1)S(1)} fusion(pred[1024,1024]{1,0:T(8,128)(4,1)} %iota_compare_fusion, bf16[2,1024,128]{2,1,0:T(8,128)(2,1)S(1)} %bitcast.156, bf16[2,1024,128]{2,1,0:T(8,128)(2,1)S(1)} %bitcast.153), kind=kOutput, calls=%fused_computation.1 | convolution fusion | flops 541065216 | bytes 6291456 | tf_op jit(solution)/shard_map/blhd,bmhd->bhlm/dot_general | solution.py:40
  68.2 1.9 copy-done.1
  70.1 2.3 convolution_bitcast_fusion.2
  72.4 43.6 %all-gather.5.cloned.1.call-done = f32[32,128,128]{2,1,0:T(8,128)} async-done(((f32[1,128,128]{2,1,0:T(8,128)}), f32[32,128,128]{2,1,0:T(8,128)}) %all-gather.5.cloned.1.call-update) | async-done | bytes 2097168 | tf_op jit(solution)/shard_map/all_gather | solution.py:33
  116.1 1.8 fusion.1
  117.9 0.0 copy-start.9
  117.9 2.3 multiply_reduce_fusion
  120.2 0.6 fusion.7
  120.8 1.0 fusion.11
  121.8 0.0 copy-done.9
  121.8 0.4 convolution_bitcast_fusion.3
  122.2 0.7 copy.92
  123.0 0.0 all-gather.7.cloned.1.call-update
  123.0 1.1 bitcast_convert_fusion
  124.1 6.7 %all-to-all-start.3 = ((bf16[16,128,128]{2,1,0:T(8,128)(2,1)}), bf16[16,128,128]{2,1,0:T(8,128)(2,1)S(1)}, u32[]{:S(2)}, u32[]{:S(2)}) async-start(bf16[16,128,128]{2,1,0:T(8,128)(2,1)} %bitcast.17), calls=%async_computation.3 | async-start | bytes 1048576 | tf_op jit(solution)/shard_map/all_to_all | solution.py:56
  130.8 2.8 %select_convert_fusion = bf16[2,1024,1024]{2,1,0:T(8,128)(2,1)S(1)} fusion(pred[1024,1024]{1,0:T(8,128)(4,1)} %iota_compare_fusion, bf16[2,1024,128]{2,1,0:T(8,128)(2,1)S(1)} %fusion.11, bf16[2,1024,128]{2,1,0:T(8,128)(2,1)} %bitcast.150), kind=kOutput, calls=%fused_computation | convolution fusion | flops 541065216 | bytes 6291456 | tf_op jit(solution)/shard_map/blhe,bmhe->bhlm/dot_general | solution.py:70
  133.7 2.0 copy-done.3
  135.7 1.2 convolution_bitcast_fusion.1
  136.9 1.4 fusion.3
  138.4 0.8 fusion.19
  139.2 0.0 copy-start.10
  139.2 2.5 %all-to-all-done.3 = bf16[16,128,128]{2,1,0:T(8,128)(2,1)S(1)} async-done(((bf16[16,128,128]{2,1,0:T(8,128)(2,1)}), bf16[16,128,128]{2,1,0:T(8,128)(2,1)S(1)}, u32[]{:S(2)}, u32[]{:S(2)}) %all-to-all-start.3) | async-done | bytes 524320 | tf_op jit(solution)/shard_map/all_to_all | solution.py:56
  141.7 4.5 %all-to-all-start.5 = ((bf16[16,128,128]{2,1,0:T(8,128)(2,1)}), bf16[16,128,128]{2,1,0:T(8,128)(2,1)}, u32[]{:S(2)}, u32[]{:S(2)}) async-start(bf16[16,128,128]{2,1,0:T(8,128)(2,1)} %bitcast.26), calls=%async_computation.5 | async-start | bytes 1048576 | tf_op jit(solution)/shard_map/all_to_all | solution.py:97
  146.1 45.9 %all-gather.7.cloned.1.call-done = f32[32,128,128]{2,1,0:T(8,128)} async-done(((f32[1,128,128]{2,1,0:T(8,128)}), f32[32,128,128]{2,1,0:T(8,128)}) %all-gather.7.cloned.1.call-update) | async-done | bytes 2097168 | tf_op jit(solution)/shard_map/all_gather | solution.py:65
  192.1 1.8 fusion
  193.9 0.1 copy.93
  194.0 0.6 fusion.6
  194.6 0.0 copy-start.5
  194.6 1.0 copy.99
  195.6 0.0 all-to-all-done.5
  195.6 6.6 %all-to-all-start.7 = ((bf16[16,128,128]{2,1,0:T(8,128)(2,1)}), bf16[16,128,128]{2,1,0:T(8,128)(2,1)S(1)}, u32[]{:S(2)}, u32[]{:S(2)}) async-start(bf16[16,128,128]{2,1,0:T(8,128)(2,1)} %bitcast.41), calls=%async_computation.7 | async-start | bytes 1048576 | tf_op jit(solution)/shard_map/all_to_all | solution.py:99
  202.2 0.0 copy-start.13
  202.2 4.0 %convolution_bitcast_fusion = f32[2,128,1024]{1,2,0:T(8,128)S(1)} fusion(bf16[2,1024,1024]{2,1,0:T(8,128)(2,1)} %copy-done.3, bf16[2,1024,128]{2,1,0:T(8,128)(2,1)S(1)} %bitcast.159), kind=kOutput, calls=%fused_computation.9 | convolution fusion | flops 536870912 | bytes 5767168 | tf_op jit(solution)/shard_map/bhlm,blhd->bmhd/dot_general | solution.py:78
  206.2 1.4 fusion.4
  207.6 5.4 %all-to-all-done.7 = bf16[16,128,128]{2,1,0:T(8,128)(2,1)S(1)} async-done(((bf16[16,128,128]{2,1,0:T(8,128)(2,1)}), bf16[16,128,128]{2,1,0:T(8,128)(2,1)S(1)}, u32[]{:S(2)}, u32[]{:S(2)}) %all-to-all-start.7) | async-done | bytes 524320 | tf_op jit(solution)/shard_map/all_to_all | solution.py:99
  213.0 3.6 %all-to-all-start.6 = ((bf16[16,128,128]{2,1,0:T(8,128)(2,1)}), bf16[16,128,128]{2,1,0:T(8,128)(2,1)S(1)}, u32[]{:S(2)}, u32[]{:S(2)}) async-start(bf16[16,128,128]{2,1,0:T(8,128)(2,1)} %bitcast.37), calls=%async_computation.6 | async-start | bytes 1048576 | tf_op jit(solution)/shard_map/all_to_all | solution.py:98
  216.6 0.9 copy_bitcast_fusion.2
  217.5 1.9 copy_bitcast_fusion.1
  219.4 0.3 copy.100
  219.7 1.0 copy.101
  220.7 5.9 %all-to-all-done.6 = bf16[16,128,128]{2,1,0:T(8,128)(2,1)S(1)} async-done(((bf16[16,128,128]{2,1,0:T(8,128)(2,1)}), bf16[16,128,128]{2,1,0:T(8,128)(2,1)S(1)}, u32[]{:S(2)}, u32[]{:S(2)}) %all-to-all-start.6) | async-done | bytes 524320 | tf_op jit(solution)/shard_map/all_to_all | solution.py:98
  226.6 0.9 copy_bitcast_fusion
  (28 shorter events, 0.1 us)
Async XLA Ops:
  7.2 1.0 copy-start
  7.2 31.3 %copy-start.14 = (bf16[128,2048]{1,0:T(8,128)(2,1)S(1)}, bf16[128,2048]{1,0:T(8,128)(2,1)}, u32[]{:S(2)}) copy-start(bf16[128,2048]{1,0:T(8,128)(2,1)} %param.7) | copy-start | bytes 1572868
  8.2 34.8 %copy-start.15 = (bf16[128,2048]{1,0:T(8,128)(2,1)S(1)}, bf16[128,2048]{1,0:T(8,128)(2,1)}, u32[]{:S(2)}) copy-start(bf16[128,2048]{1,0:T(8,128)(2,1)} %param.4) | copy-start | bytes 1572868
  9.1 16.6 %all-to-all-start.1 = ((bf16[128,16,128]{2,0,1:T(8,128)(2,1)}), bf16[128,16,128]{2,0,1:T(8,128)(2,1)S(1)}, u32[]{:S(2)}, u32[]{:S(2)}) async-start(bf16[128,16,128]{2,0,1:T(8,128)(2,1)} %copy_bitcast_fusion.5), calls=%async_computation.1 | async-start | bytes 1048576 | tf_op jit(solution)/shard_map/all_to_all | solution.py:15
  16.7 99.3 %all-gather.5.cloned.1.call-start = ((), (), s32[]{:S(2)}) async-start(), calls=%async_computation.8 | async-start | bytes 2162688 | tf_op jit(solution)/shard_map/all_gather | solution.py:33
  25.7 39.5 %copy-start.6 = (bf16[128,16,128]{2,0,1:T(8,128)(2,1)}, bf16[128,16,128]{2,0,1:T(8,128)(2,1)S(1)}, u32[]{:S(2)}) copy-start(bf16[128,16,128]{2,0,1:T(8,128)(2,1)S(1)} %all-to-all-done.1) | copy-start | bytes 1572868
  37.5 30.7 %copy-start.4 = (bf16[128,16,128]{2,0,1:T(8,128)(2,1)}, bf16[128,16,128]{2,0,1:T(8,128)(2,1)S(1)}, u32[]{:S(2)}) copy-start(bf16[128,16,128]{2,0,1:T(8,128)(2,1)S(1)} %all_to_all.137) | copy-start | bytes 1572868
  39.4 12.5 %all-to-all-start.4 = ((bf16[128,16,128]{2,0,1:T(8,128)(2,1)}), bf16[128,16,128]{2,0,1:T(8,128)(2,1)S(1)}, u32[]{:S(2)}, u32[]{:S(2)}) async-start(bf16[128,16,128]{2,0,1:T(8,128)(2,1)} %copy_bitcast_fusion.3), calls=%async_computation.4 | async-start | bytes 1048576 | tf_op jit(solution)/shard_map/all_to_all | solution.py:17
  52.0 0.8 copy-start.11
  52.8 12.5 %all-to-all-start = ((bf16[128,16,128]{2,0,1:T(8,128)(2,1)}), bf16[128,16,128]{2,0,1:T(8,128)(2,1)S(1)}, u32[]{:S(2)}, u32[]{:S(2)}) async-start(bf16[128,16,128]{2,0,1:T(8,128)(2,1)} %copy_bitcast_fusion.6), calls=%async_computation | async-start | bytes 1048576 | tf_op jit(solution)/shard_map/all_to_all | solution.py:14
  56.3 135.7 %all-gather.7.cloned.1.call-start = ((), (), s32[]{:S(2)}) async-start(), calls=%async_computation.9 | async-start | bytes 2162688 | tf_op jit(solution)/shard_map/all_gather | solution.py:65
  65.3 7.1 %copy-start.8 = (bf16[128,16,128]{2,0,1:T(8,128)(2,1)}, bf16[128,16,128]{2,0,1:T(8,128)(2,1)S(1)}, u32[]{:S(2)}) copy-start(bf16[128,16,128]{2,0,1:T(8,128)(2,1)S(1)} %all-to-all-done) | copy-start | bytes 1572868
  68.2 1.9 copy-start.1
  117.9 4.0 %copy-start.9 = (bf16[128,16,128]{2,0,1:T(8,128)(2,1)S(1)}, bf16[128,16,128]{2,0,1:T(8,128)(2,1)}, u32[]{:S(2)}) copy-start(bf16[128,16,128]{2,0,1:T(8,128)(2,1)} %copy-done.8) | copy-start | bytes 1572868
  124.1 11.6 %copy-start.7 = (bf16[128,16,128]{2,0,1:T(8,128)(2,1)S(1)}, bf16[128,16,128]{2,0,1:T(8,128)(2,1)}, u32[]{:S(2)}) copy-start(bf16[128,16,128]{2,0,1:T(8,128)(2,1)} %copy-done.6) | copy-start | bytes 1572868
  124.1 17.6 %all-to-all-start.3 = ((bf16[16,128,128]{2,1,0:T(8,128)(2,1)}), bf16[16,128,128]{2,1,0:T(8,128)(2,1)S(1)}, u32[]{:S(2)}, u32[]{:S(2)}) async-start(bf16[16,128,128]{2,1,0:T(8,128)(2,1)} %bitcast.17), calls=%async_computation.3 | async-start | bytes 1048576 | tf_op jit(solution)/shard_map/all_to_all | solution.py:56
  133.7 2.0 copy-start.3
  135.7 2.7 %copy-start.2 = (bf16[2,1024,1024]{2,1,0:T(8,128)(2,1)S(1)}, bf16[2,1024,1024]{2,1,0:T(8,128)(2,1)}, u32[]{:S(2)}) copy-start(bf16[2,1024,1024]{2,1,0:T(8,128)(2,1)} %copy-done.1) | copy-start | bytes 12582916
  139.2 63.0 %copy-start.10 = (bf16[128,16,128]{2,0,1:T(8,128)(2,1)S(1)}, bf16[128,16,128]{2,0,1:T(8,128)(2,1)}, u32[]{:S(2)}) copy-start(bf16[128,16,128]{2,0,1:T(8,128)(2,1)} %copy-done.8) | copy-start | bytes 1572868
  141.7 52.3 %copy-start.12 = (bf16[16,128,128]{2,1,0:T(8,128)(2,1)}, bf16[16,128,128]{2,1,0:T(8,128)(2,1)S(1)}, u32[]{:S(2)}) copy-start(bf16[16,128,128]{2,1,0:T(8,128)(2,1)S(1)} %all-to-all-done.3) | copy-start | bytes 1572868
  141.7 53.9 %all-to-all-start.5 = ((bf16[16,128,128]{2,1,0:T(8,128)(2,1)}), bf16[16,128,128]{2,1,0:T(8,128)(2,1)}, u32[]{:S(2)}, u32[]{:S(2)}) async-start(bf16[16,128,128]{2,1,0:T(8,128)(2,1)} %bitcast.26), calls=%async_computation.5 | async-start | bytes 1048576 | tf_op jit(solution)/shard_map/all_to_all | solution.py:97
  194.6 11.6 %copy-start.5 = (bf16[128,16,128]{2,0,1:T(8,128)(2,1)S(1)}, bf16[128,16,128]{2,0,1:T(8,128)(2,1)}, u32[]{:S(2)}) copy-start(bf16[128,16,128]{2,0,1:T(8,128)(2,1)} %copy-done.4) | copy-start | bytes 1572868
  195.6 17.4 %all-to-all-start.7 = ((bf16[16,128,128]{2,1,0:T(8,128)(2,1)}), bf16[16,128,128]{2,1,0:T(8,128)(2,1)S(1)}, u32[]{:S(2)}, u32[]{:S(2)}) async-start(bf16[16,128,128]{2,1,0:T(8,128)(2,1)} %bitcast.41), calls=%async_computation.7 | async-start | bytes 1048576 | tf_op jit(solution)/shard_map/all_to_all | solution.py:99
  202.2 14.4 %copy-start.13 = (bf16[16,128,128]{2,1,0:T(8,128)(2,1)S(1)}, bf16[16,128,128]{2,1,0:T(8,128)(2,1)}, u32[]{:S(2)}) copy-start(bf16[16,128,128]{2,1,0:T(8,128)(2,1)} %copy-done.12) | copy-start | bytes 1572868
  213.0 13.6 %all-to-all-start.6 = ((bf16[16,128,128]{2,1,0:T(8,128)(2,1)}), bf16[16,128,128]{2,1,0:T(8,128)(2,1)S(1)}, u32[]{:S(2)}, u32[]{:S(2)}) async-start(bf16[16,128,128]{2,1,0:T(8,128)(2,1)} %bitcast.37), calls=%async_computation.6 | async-start | bytes 1048576 | tf_op jit(solution)/shard_map/all_to_all | solution.py:98
Sparse Core Ops, SparseCore 0:
  38.6 77.4 all-gather.4
  123.1 68.9 all-gather.6
where the time goes:
time: 236 us; the launch traced here: 234 us
  waiting for transfers between devices  126 us (53%)
  starting transfers between devices  36.1 us (15%)
  matrix products  20.4 us (9%)
  local copies, waits for them, and re-layouts  16.5 us (7%)
  between operations  14.4 us (6%)
  blocking collectives  11.7 us (5%)
  other arithmetic  9.45 us (4%)
    all_gather x1, waiting for transfers between devices, shards(): shard_block = lax.all_gather(device_grad[None], 'seq', axis=0, tiled=True)  45.9 us
    all_gather x1, waiting for transfers between devices, shards(): shard_block = lax.all_gather(device_kv[None], 'seq', axis=0, tiled=True)  43.6 us
    all_to_all x1, blocking collectives, shards(): lax.all_to_all(value_vectors, 'head', split_axis=1, concat_axis=0, tiled=...  11.7 us
    all_to_all x1, waiting for transfers between devices, shards(): lax.all_to_all(cotangent, 'head', split_axis=1, concat_axis=0, tiled=True)  8.01 us
    all_to_all x1, waiting for transfers between devices, shards(): lax.all_to_all(key_vectors, 'head', split_axis=1, concat_axis=0, tiled=True)  7.78 us
    all_to_all x1, starting transfers between devices, shards(): lax.all_to_all(key_vectors, 'head', split_axis=1, concat_axis=0, tiled=True)  7.58 us
    unnamed x33, local copies, waits for them, and re-layouts  6.83 us
    all_to_all x1, starting transfers between devices, shards(): lax.all_to_all(normed_bf, 'head', split_axis=0, concat_axis=1, tiled=True)  6.72 us
  transfers between devices with their start and end apart: 9, of which 8 were waited for; matrix products, arithmetic and copies ran while one was open for 13% of the time, Pallas kernels for 0%

commit v1 on v0

v1 whole, which is shorter than its diff:
```python
import jax
import jax.numpy as jnp
from jax import lax
from jax.experimental import pallas as pl
from jax.experimental.pallas import tpu as pltpu
from jax.sharding import PartitionSpec as P

N = 16
DH = 128
GROUPS = 4
MEMBERS = 8
EPS = 1e-06
UNROLL = 4
MESH = pl.DeviceIdType.MESH
F32 = jnp.float32
BF16 = jnp.bfloat16


def dot(a, b, ca, cb):
    return lax.dot_general(a, b, (((ca,), (cb,)), ((), ())), preferred_element_type=F32)


def kernel(
    q_hbm, k_hbm, v_hbm, g_hbm,
    n_hbm, qg_hbm, kg_hbm, vg_hbm,
    q_v, k_v, v_v, g_v,
    kv_s, kv_r, a_s, a_r, q_r, g_r,
    p_s, p_r, t_s, t_r,
    sc_v, al_v, sg_v, kl_v, vl_v,
    n_v, qg_v, kg_v, vg_v,
    za, zb, zc, zd, ze,
    in_sem, out_sem, self_sem, send_sem, recv_sem, zsend_sem, z1_sem, z2_sem, z3_sem,
):
    me = lax.axis_index("head")
    seq = lax.axis_index("seq")
    group = seq // MEMBERS
    member = seq % MEMBERS

    def plane(i):
        return (i, seq)

    def column(m):
        return (me, group * MEMBERS + m)

    def across(g):
        return (me, g * MEMBERS + member)

    def turn(j):
        return lax.rem(me + j, N)

    def cols(h):
        return pl.ds(pl.multiple_of(h * DH, DH), DH)

    barrier = pltpu.get_barrier_semaphore()
    loads = [
        pltpu.make_async_copy(src, dst, in_sem.at[i])
        for i, (src, dst) in enumerate(((k_hbm, k_v), (v_hbm, v_v), (q_hbm, q_v), (g_hbm, g_v)))
    ]
    for load in loads:
        load.start()

    @pl.loop(1, N)
    def _(j):
        pl.semaphore_signal(barrier, inc=1, device_id=plane(turn(j)), device_id_type=MESH)

    for j in range(1, MEMBERS):
        pl.semaphore_signal(
            barrier, inc=1, device_id=column(lax.rem(member + j, MEMBERS)), device_id_type=MESH
        )
    for j in range(1, GROUPS):
        pl.semaphore_signal(
            barrier, inc=1, device_id=across(lax.rem(group + j, GROUPS)), device_id_type=MESH
        )

    def send(which, src, dst, to):
        return pltpu.make_async_remote_copy(
            src_ref=src,
            dst_ref=dst,
            send_sem=send_sem.at[which],
            recv_sem=recv_sem.at[which, me],
            device_id=plane(to),
            device_id_type=MESH,
        )

    def arrived(which, buf, src):
        pltpu.make_async_remote_copy(
            src_ref=buf.at[src],
            dst_ref=buf.at[src],
            send_sem=send_sem.at[which],
            recv_sem=recv_sem.at[which, src],
            device_id=plane(me),
            device_id_type=MESH,
        ).wait_recv()

    def all_sent(which, buf):
        pltpu.make_async_copy(
            buf.at[pl.ds(0, N - 1)], buf.at[pl.ds(0, N - 1)], send_sem.at[which]
        ).wait()

    loads[0].wait()
    loads[1].wait()

    @pl.loop(0, N // UNROLL)
    def _(t):
        for u in range(UNROLL):
            h = turn(t * UNROLL + u + 1)
            kv_s[h] = dot(k_v[:, cols(h)], v_v[:, cols(h)], 0, 0).astype(BF16)

    kv_r[me] = kv_s[me]
    pl.semaphore_wait(barrier, N - 1 + MEMBERS - 1 + GROUPS - 1)

    @pl.loop(1, N)
    def _(j):
        h = turn(j)
        send(0, kv_s.at[h], kv_r.at[me], h).start()

    loads[2].wait()
    loads[3].wait()
    mine_q = pltpu.make_async_copy(q_v.at[:, cols(me)], q_r.at[me], self_sem.at[0])
    mine_g = pltpu.make_async_copy(g_v.at[:, cols(me)], g_r.at[me], self_sem.at[1])
    mine_q.start()
    mine_g.start()

    @pl.loop(1, N)
    def _(j):
        h = turn(j)
        send(1, q_v.at[:, cols(h)], q_r.at[me], h).start()
        send(2, g_v.at[:, cols(h)], g_r.at[me], h).start()

    rows = lax.broadcasted_iota(jnp.int32, (DH, DH), 0)
    causal = rows >= lax.broadcasted_iota(jnp.int32, (DH, DH), 1)

    @pl.loop(0, N // UNROLL)
    def _(t):
        for u in range(UNROLL):
            h = turn(t * UNROLL + u + 1)
            scores = dot(q_v[:, cols(h)], k_v[:, cols(h)], 1, 1)
            scores = jnp.where(causal, scores, F32(0.0)).astype(BF16)
            sc_v[h] = scores
            local = dot(scores, v_v[:, cols(h)], 1, 0)
            al_v[h] = local
            a_s[h] = local.astype(BF16)

        for u in range(UNROLL):
            j = t * UNROLL + u + 1
            h = turn(j)

            @pl.when(j < N)
            def _():
                send(3, a_s.at[h], a_r.at[me], h).start()

    a_r[me] = a_s[me]

    def exchange(first, reverse, totals):
        z = 1 if reverse else 0

        def zsend(step, src, dst, sem, to):
            return pltpu.make_async_remote_copy(
                src_ref=src,
                dst_ref=dst,
                send_sem=zsend_sem.at[z, step],
                recv_sem=sem,
                device_id=to,
                device_id_type=MESH,
            )

        def zwait(dst, sem):
            pltpu.make_async_copy(dst, dst, sem).wait()

        za[z] = totals.reshape(MEMBERS, DH // MEMBERS, DH)
        for j in range(1, MEMBERS):
            m = lax.rem(member + j, MEMBERS)
            zsend(0, za.at[z, m], zb.at[z, member], z1_sem.at[z, member], column(m)).start()
        zb[z, member] = za[z, member]
        first()
        for j in range(1, MEMBERS):
            m = lax.rem(member + j, MEMBERS)
            zwait(zb.at[z, m], z1_sem.at[z, m])
        total = zb[z, 0]
        for m in range(1, MEMBERS):
            total += zb[z, m]
        zc[z, GROUPS] = total
        zc[z, group] = jnp.zeros_like(total)
        for j in range(1, GROUPS):
            g = lax.rem(group + j, GROUPS)
            zsend(1, zc.at[z, GROUPS], zc.at[z, group], z2_sem.at[z, group], across(g)).start()
        for j in range(1, GROUPS):
            g = lax.rem(group + j, GROUPS)
            zwait(zc.at[z, g], z2_sem.at[z, g])
        running = jnp.zeros_like(total)
        for g in range(GROUPS):
            counts = (g > group) if reverse else (g < group)
            running += jnp.where(counts, zc[z, g], F32(0.0))
        for m in range(MEMBERS):
            m = MEMBERS - 1 - m if reverse else m
            zd[z, m] = running
            running += zb[z, m]
        for j in range(1, MEMBERS):
            m = lax.rem(member + j, MEMBERS)
            zsend(2, zd.at[z, m], ze.at[z, member], z3_sem.at[z, member], column(m)).start()
        ze[z, member] = zd[z, member]
        for j in range(1, MEMBERS):
            m = lax.rem(member + j, MEMBERS)
            zwait(ze.at[z, m], z3_sem.at[z, m])
        return ze[z].reshape(DH, DH)

    def exchange_sent(z):
        pltpu.make_async_copy(
            za.at[z, pl.ds(0, MEMBERS - 1)], za.at[z, pl.ds(0, MEMBERS - 1)], zsend_sem.at[z, 0]
        ).wait()
        pltpu.make_async_copy(
            zc.at[z, pl.ds(0, GROUPS - 1)], zc.at[z, pl.ds(0, GROUPS - 1)], zsend_sem.at[z, 1]
        ).wait()
        pltpu.make_async_copy(
            zd.at[z, pl.ds(0, MEMBERS - 1)], zd.at[z, pl.ds(0, MEMBERS - 1)], zsend_sem.at[z, 2]
        ).wait()

    @pl.loop(1, N)
    def _(j):
        arrived(0, kv_r, turn(j))

    total = kv_r[0].astype(F32)
    for i in range(1, N):
        total += kv_r[i].astype(F32)
    state = exchange(lambda: None, False, total)
    for i in range(N):
        p_s[i] = state.astype(BF16)
        state += kv_r[i].astype(F32)
    p_r[me] = p_s[me]

    mine_q.wait()
    mine_g.wait()

    @pl.loop(1, N)
    def _(j):
        i = turn(j)
        arrived(1, q_r, i)
        arrived(2, g_r, i)
        arrived(3, a_r, i)

    def normalize(attn, cot):
        inv_rms = lax.rsqrt(jnp.mean(attn * attn, axis=-1, keepdims=True) + EPS)
        normed = attn * inv_rms
        cot = cot.astype(F32)
        along = jnp.mean(cot * normed, axis=-1, keepdims=True)
        return normed, (inv_rms * (cot - normed * along)).astype(BF16)

    @pl.loop(0, N // UNROLL)
    def _(t):
        for u in range(UNROLL):
            i = t * UNROLL + u
            q = q_r[i]
            attn = a_r[i].astype(F32) + dot(q, p_s[i], 1, 0)
            _, out_grad = normalize(attn, g_r[i])
            sg_v[i] = dot(q, out_grad, 0, 0)

    total = sg_v[0]
    for i in range(1, N):
        total += sg_v[i]

    def send_states():
        @pl.loop(1, N)
        def _(j):
            i = turn(j)
            send(4, p_s.at[i], p_r.at[me], i).start()

    later = exchange(send_states, True, total)
    for i in range(N - 1, -1, -1):
        t_s[i] = later.astype(BF16)
        later += sg_v[i]
    t_r[me] = t_s[me]

    @pl.loop(1, N)
    def _(j):
        i = turn(j)
        send(5, t_s.at[i], t_r.at[me], i).start()

    @pl.loop(1, N)
    def _(j):
        arrived(4, p_r, turn(j))

    @pl.loop(0, N // UNROLL)
    def _(t):
        for u in range(UNROLL):
            h = t * UNROLL + u
            c = cols(h)
            q = q_v[:, c]
            state = p_r[h]
            attn = al_v[h] + dot(q, state, 1, 0)
            normed, out_grad = normalize(attn, g_v[:, c])
            n_v[:, c] = normed.astype(BF16)
            grads = dot(out_grad, v_v[:, c], 1, 1)
            grads = jnp.where(causal, grads, F32(0.0)).astype(BF16)
            query_grad = dot(grads, k_v[:, c], 1, 0) + dot(out_grad, state, 1, 1)
            qg_v[:, c] = query_grad.astype(BF16)
            kl_v[h] = dot(grads, q, 0, 0)
            vl_v[h] = dot(sc_v[h], out_grad, 0, 0)

    stores = [
        pltpu.make_async_copy(src, dst, out_sem.at[i])
        for i, (src, dst) in enumerate(
            ((n_v, n_hbm), (qg_v, qg_hbm), (kg_v, kg_hbm), (vg_v, vg_hbm))
        )
    ]
    stores[0].start()
    stores[1].start()

    @pl.loop(1, N)
    def _(j):
        arrived(5, t_r, turn(j))

    @pl.loop(0, N // UNROLL)
    def _(t):
        for u in range(UNROLL):
            h = t * UNROLL + u
            c = cols(h)
            grad_state = t_r[h]
            kg_v[:, c] = (kl_v[h] + dot(v_v[:, c], grad_state, 1, 1)).astype(BF16)
            vg_v[:, c] = (vl_v[h] + dot(k_v[:, c], grad_state, 1, 0)).astype(BF16)

    stores[2].start()
    stores[3].start()
    for which, buf in enumerate((kv_s, q_r, g_r, a_s, p_s, t_s)):
        all_sent(which, buf)
    exchange_sent(0)
    exchange_sent(1)
    for store in stores:
        store.wait()


def shards(q, k, v, g):
    tokens, width = q.shape
    wide = pltpu.VMEM((tokens, width), BF16)
    blocks = pltpu.VMEM((N, DH, DH), BF16)
    sums = pltpu.VMEM((N, DH, DH), F32)
    eighths = pltpu.VMEM((2, MEMBERS, DH // MEMBERS, DH), F32)
    groups = pltpu.VMEM((2, GROUPS + 1, DH // MEMBERS, DH), F32)
    dma = pltpu.SemaphoreType.DMA
    return pl.pallas_call(
        kernel,
        out_shape=[jax.ShapeDtypeStruct((tokens, width), BF16)] * 4,
        in_specs=[pl.BlockSpec(memory_space=pl.ANY)] * 4,
        out_specs=[pl.BlockSpec(memory_space=pl.ANY)] * 4,
        scratch_shapes=[wide] * 4
        + [blocks] * 10
        + [blocks] + [sums] * 4
        + [wide] * 4
        + [eighths, eighths, groups, eighths, eighths]
        + [dma((4,)), dma((4,)), dma((2,)), dma((6,)), dma((6, N))]
        + [dma((2, 3)), dma((2, MEMBERS)), dma((2, GROUPS)), dma((2, MEMBERS))],
        compiler_params=pltpu.CompilerParams(
            collective_id=0, has_side_effects=True, vmem_limit_bytes=60 * 1024 * 1024
        ),
        cost_estimate=pl.CostEstimate(
            flops=2 * 14 * N * DH**3, bytes_accessed=16 * tokens * width, transcendentals=0
        ),
    )(q, k, v, g)


def solution(mesh):
    spec = P(("seq", "head"), None)
    return jax.shard_map(
        shards, mesh=mesh, in_specs=(spec,) * 4, out_specs=(spec,) * 4, check_vma=False
    )
```

time: 236 us -> 83.1 us (0.35)
  waiting for transfers between devices: 126 us -> 0 us
  Pallas kernels: 0 us -> 76.9 us
  starting transfers between devices: 36.1 us -> 0 us
  matrix products: 20.4 us -> 0 us
  between operations: 14.4 us -> 0.65 us
  blocking collectives: 11.7 us -> 0 us
  local copies, waits for them, and re-layouts: 16.5 us -> 5.19 us
  other arithmetic: 9.45 us -> 0 us
    all_gather x2 -> x0, waiting for transfers between devices: 89.6 us -> none  [the longest x1 45.9 us: shards(): shard_block = lax.all_gather(device_grad[None], 'seq', axis=0, tiled=True)]
    pallas_call x0 -> x1, Pallas kernels: none -> 76.9 us  [shards(): pl.pallas_call(kernel, out_shape=[jax.ShapeDtypeStruct((tokens, width), B...]
    all_to_all x7 -> x0, waiting for transfers between devices: 36.1 us -> none  [the longest x1 8.01 us: shards(): lax.all_to_all(cotangent, 'head', split_axis=1, concat_axis=0, tiled=True)]
    all_to_all x7 -> x0, starting transfers between devices: 36 us -> none  [the longest x1 7.58 us: shards(): lax.all_to_all(key_vectors, 'head', split_axis=1, concat_axis=0, tiled=True)]
    dot_general x12 -> x0, matrix products: 20.4 us -> none  [the longest x1 3.97 us: shards(): jnp.einsum('bhlm,blhd->bmhd', masked_grads, query_heads, preferred_elemen...]
    all_to_all x1 -> x0, blocking collectives: 11.7 us -> none  [shards(): lax.all_to_all(value_vectors, 'head', split_axis=1, concat_axis=0, tiled=...]
    all_to_all x8 -> x0, local copies, waits for them, and re-layouts: 7.89 us -> none  [the longest x1 1.91 us: shards(): lax.all_to_all(query_bf, 'head', split_axis=0, concat_axis=1, tiled=True)]
    reduce_sum x3 -> x0, other arithmetic: 4.24 us -> none  [the longest x1 1.8 us: shards(): suffix = jnp.sum(later[:, None, None, None] * shard_block, axis=0)]
  transfers between devices with their start and end apart: 9 -> 0, of which waited for: 8 -> 0; matrix products, arithmetic and copies ran while one was open for 13% -> 0% of each run, Pallas kernels for 0% -> 0%
where the time goes in v1:
time: 83.1 us; the launch traced here: 82.7 us
  Pallas kernels  76.9 us (93%)
  local copies, waits for them, and re-layouts  5.19 us (6%)
    pallas_call x1, Pallas kernels, shards(): pl.pallas_call(kernel, out_shape=[jax.ShapeDtypeStruct((tokens, width), B...  76.9 us
    unnamed x10, local copies, waits for them, and re-layouts  5.19 us

profile of v1, /device:TPU:1, one launch (start us, length us, event | category | flops | bytes accessed | tf_op | source)
XLA Modules:
  0.0 82.7 jit_solution(9200364795307312974)
XLA Ops:
  0.6 76.9 %shard_map.75 = (bf16[128,2048]{1,0:T(8,128)(2,1)}, bf16[128,2048]{1,0:T(8,128)(2,1)}, bf16[128,2048]{1,0:T(8,128)(2,1)}, bf16[128,2048]{1,0:T(8,128)(2,1)}) custom-call(bf16[128,2048]{1,0:T(8,128)(2,1)} %q_hbm.1, bf16[128,2048]{1,0:T(8,128)(2,1)} %k_hbm.1, bf16[128,2048]{1,0:T(8,128)(2,1)} %v_hbm.1, bf16[128,2048]{1,0:T(8,128)(2,1)} %g_hbm.1), custom_call_target="tpu_custom_call" | custom-call | flops 939524096 | bytes 4194304 | tf_op jit(solution)/shard_map/pallas_call | solution.py:339
  77.5 0.0 copy-start.2
  77.5 1.9 %copy.12 = bf16[128,2048]{1,0:T(8,128)(2,1)} copy(bf16[128,2048]{1,0:T(8,128)(2,1)} %get-tuple-element.8) | data formatting | bytes 1048576
  79.5 0.0 copy-done.2
  79.5 0.0 copy-start.1
  79.5 0.8 copy.13
  80.3 0.4 copy-done.1
  80.7 0.0 copy-start
  80.7 0.8 copy.14
  81.5 0.4 copy-done
  81.9 0.8 copy.15
Async XLA Ops:
  77.5 2.0 %copy-start.2 = (bf16[128,2048]{1,0:T(8,128)(2,1)S(1)}, bf16[128,2048]{1,0:T(8,128)(2,1)}, u32[]{:S(2)}) copy-start(bf16[128,2048]{1,0:T(8,128)(2,1)} %get-tuple-element.9) | copy-start | bytes 1572868
  79.5 1.2 %copy-start.1 = (bf16[128,2048]{1,0:T(8,128)(2,1)S(1)}, bf16[128,2048]{1,0:T(8,128)(2,1)}, u32[]{:S(2)}) copy-start(bf16[128,2048]{1,0:T(8,128)(2,1)} %get-tuple-element.10) | copy-start | bytes 1572868
  80.7 1.2 %copy-start = (bf16[128,2048]{1,0:T(8,128)(2,1)S(1)}, bf16[128,2048]{1,0:T(8,128)(2,1)}, u32[]{:S(2)}) copy-start(bf16[128,2048]{1,0:T(8,128)(2,1)} %get-tuple-element.11) | copy-start | bytes 1572868

commit v2 on v1

--- a/solution.py
+++ b/solution.py
@@ -10,7 +10,11 @@
 GROUPS = 4
 MEMBERS = 8
 EPS = 1e-06
-UNROLL = 4
+STEPS = (
+    (2, 2), (2, 1), (1, 2), (2, 3), (3, 2), (1, 1), (3, 3), (1, 3), (3, 1),
+    (2, 0), (0, 2), (1, 0), (0, 1), (3, 0), (0, 3),
+)
+EARLY = 0
 MESH = pl.DeviceIdType.MESH
 F32 = jnp.float32
 BF16 = jnp.bfloat16
@@ -22,12 +26,12 @@
 
 def kernel(
     q_hbm, k_hbm, v_hbm, g_hbm,
-    n_hbm, qg_hbm, kg_hbm, vg_hbm,
+    n_hbm, qg_hbm, t_hbm, kl_hbm, vl_hbm,
     q_v, k_v, v_v, g_v,
     kv_s, kv_r, a_s, a_r, q_r, g_r,
-    p_s, p_r, t_s, t_r,
+    p_s, p_r, t_s,
     sc_v, al_v, sg_v, kl_v, vl_v,
-    n_v, qg_v, kg_v, vg_v,
+    n_v, qg_v,
     za, zb, zc, zd, ze,
     in_sem, out_sem, self_sem, send_sem, recv_sem, zsend_sem, z1_sem, z2_sem, z3_sem,
 ):
@@ -49,7 +53,12 @@
         return lax.rem(me + j, N)
 
     def cols(h):
+        if isinstance(h, int):
+            return pl.ds(h * DH, DH)
         return pl.ds(pl.multiple_of(h * DH, DH), DH)
+
+    y, x = me // 4, me % 4
+    others = [lax.rem(y + dy, 4) * 4 + lax.rem(x + dx, 4) for dx, dy in STEPS]
 
     barrier = pltpu.get_barrier_semaphore()
     loads = [
@@ -100,18 +109,13 @@
     loads[0].wait()
     loads[1].wait()
 
-    @pl.loop(0, N // UNROLL)
-    def _(t):
-        for u in range(UNROLL):
-            h = turn(t * UNROLL + u + 1)
-            kv_s[h] = dot(k_v[:, cols(h)], v_v[:, cols(h)], 0, 0).astype(BF16)
+    for h in range(N):
+        kv_s[h] = dot(k_v[:, cols(h)], v_v[:, cols(h)], 0, 0).astype(BF16)
 
     kv_r[me] = kv_s[me]
     pl.semaphore_wait(barrier, N - 1 + MEMBERS - 1 + GROUPS - 1)
 
-    @pl.loop(1, N)
-    def _(j):
-        h = turn(j)
+    for h in others:
         send(0, kv_s.at[h], kv_r.at[me], h).start()
 
     loads[2].wait()
@@ -121,37 +125,26 @@
     mine_q.start()
     mine_g.start()
 
-    @pl.loop(1, N)
-    def _(j):
-        h = turn(j)
+    for h in others:
         send(1, q_v.at[:, cols(h)], q_r.at[me], h).start()
+    for h in others:
         send(2, g_v.at[:, cols(h)], g_r.at[me], h).start()
 
     rows = lax.broadcasted_iota(jnp.int32, (DH, DH), 0)
     causal = rows >= lax.broadcasted_iota(jnp.int32, (DH, DH), 1)
 
-    @pl.loop(0, N // UNROLL)
-    def _(t):
-        for u in range(UNROLL):
-            h = turn(t * UNROLL + u + 1)
-            scores = dot(q_v[:, cols(h)], k_v[:, cols(h)], 1, 1)
-            scores = jnp.where(causal, scores, F32(0.0)).astype(BF16)
-            sc_v[h] = scores
-            local = dot(scores, v_v[:, cols(h)], 1, 0)
-            al_v[h] = local
-            a_s[h] = local.astype(BF16)
-
-        for u in range(UNROLL):
-            j = t * UNROLL + u + 1
-            h = turn(j)
-
-            @pl.when(j < N)
-            def _():
-                send(3, a_s.at[h], a_r.at[me], h).start()
-
+    for h in range(N):
+        scores = dot(q_v[:, cols(h)], k_v[:, cols(h)], 1, 1)
+        scores = jnp.where(causal, scores, F32(0.0)).astype(BF16)
+        sc_v[h] = scores
+        local = dot(scores, v_v[:, cols(h)], 1, 0)
+        al_v[h] = local
+        a_s[h] = local.astype(BF16)
+    for h in others:
+        send(3, a_s.at[h], a_r.at[me], h).start()
     a_r[me] = a_s[me]
 
-    def exchange(first, reverse, totals):
+    def exchange(reverse, totals, first, second):
         z = 1 if reverse else 0
 
         def zsend(step, src, dst, sem, to):
@@ -184,6 +177,7 @@
         for j in range(1, GROUPS):
             g = lax.rem(group + j, GROUPS)
             zsend(1, zc.at[z, GROUPS], zc.at[z, group], z2_sem.at[z, group], across(g)).start()
+        second()
         for j in range(1, GROUPS):
             g = lax.rem(group + j, GROUPS)
             zwait(zc.at[z, g], z2_sem.at[z, g])
@@ -222,7 +216,7 @@
     total = kv_r[0].astype(F32)
     for i in range(1, N):
         total += kv_r[i].astype(F32)
-    state = exchange(lambda: None, False, total)
+    state = exchange(False, total, lambda: None, lambda: None)
     for i in range(N):
         p_s[i] = state.astype(BF16)
         state += kv_r[i].astype(F32)
@@ -245,44 +239,22 @@
         along = jnp.mean(cot * normed, axis=-1, keepdims=True)
         return normed, (inv_rms * (cot - normed * along)).astype(BF16)
 
-    @pl.loop(0, N // UNROLL)
-    def _(t):
-        for u in range(UNROLL):
-            i = t * UNROLL + u
-            q = q_r[i]
-            attn = a_r[i].astype(F32) + dot(q, p_s[i], 1, 0)
-            _, out_grad = normalize(attn, g_r[i])
-            sg_v[i] = dot(q, out_grad, 0, 0)
+    for i in range(N):
+        q = q_r[i]
+        attn = a_r[i].astype(F32) + dot(q, p_s[i], 1, 0)
+        _, out_grad = normalize(attn, g_r[i])
+        sg_v[i] = dot(q, out_grad, 0, 0)
 
     total = sg_v[0]
     for i in range(1, N):
         total += sg_v[i]
 
     def send_states():
-        @pl.loop(1, N)
-        def _(j):
-            i = turn(j)
+        for i in others:
             send(4, p_s.at[i], p_r.at[me], i).start()
 
-    later = exchange(send_states, True, total)
-    for i in range(N - 1, -1, -1):
-        t_s[i] = later.astype(BF16)
-        later += sg_v[i]
-    t_r[me] = t_s[me]
-
-    @pl.loop(1, N)
-    def _(j):
-        i = turn(j)
-        send(5, t_s.at[i], t_r.at[me], i).start()
-
-    @pl.loop(1, N)
-    def _(j):
-        arrived(4, p_r, turn(j))
-
-    @pl.loop(0, N // UNROLL)
-    def _(t):
-        for u in range(UNROLL):
-            h = t * UNROLL + u
+    def home(heads):
+        for h in heads:
             c = cols(h)
             q = q_v[:, c]
             state = p_r[h]
@@ -296,34 +268,90 @@
             kl_v[h] = dot(grads, q, 0, 0)
             vl_v[h] = dot(sc_v[h], out_grad, 0, 0)
 
+    def early():
+        @pl.loop(1, N)
+        def _(j):
+            arrived(4, p_r, turn(j))
+
+        home(range(EARLY))
+
+    later = exchange(True, total, send_states, early)
+    for i in range(N - 1, -1, -1):
+        t_s[i] = later.astype(BF16)
+        later += sg_v[i]
+    for i in others:
+        send(5, t_s.at[i], t_hbm.at[me], i).start()
+    mine_t = pltpu.make_async_copy(t_s.at[me], t_hbm.at[me], self_sem.at[2])
+    mine_t.start()
+    home(range(EARLY, N))
+
     stores = [
         pltpu.make_async_copy(src, dst, out_sem.at[i])
         for i, (src, dst) in enumerate(
-            ((n_v, n_hbm), (qg_v, qg_hbm), (kg_v, kg_hbm), (vg_v, vg_hbm))
+            ((n_v, n_hbm), (qg_v, qg_hbm), (kl_v, kl_hbm), (vl_v, vl_hbm))
         )
     ]
-    stores[0].start()
-    stores[1].start()
+    for store in stores:
+        store.start()
 
     @pl.loop(1, N)
     def _(j):
-        arrived(5, t_r, turn(j))
-
-    @pl.loop(0, N // UNROLL)
-    def _(t):
-        for u in range(UNROLL):
-            h = t * UNROLL + u
-            c = cols(h)
-            grad_state = t_r[h]
-            kg_v[:, c] = (kl_v[h] + dot(v_v[:, c], grad_state, 1, 1)).astype(BF16)
-            vg_v[:, c] = (vl_v[h] + dot(k_v[:, c], grad_state, 1, 0)).astype(BF16)
-
-    stores[2].start()
-    stores[3].start()
+        arrived(5, t_hbm, turn(j))
+
+    mine_t.wait()
     for which, buf in enumerate((kv_s, q_r, g_r, a_s, p_s, t_s)):
         all_sent(which, buf)
     exchange_sent(0)
     exchange_sent(1)
+    for store in stores:
+        store.wait()
+
+
+def finish(
+    n_hbm, qg_hbm, t_hbm, kl_hbm, vl_hbm, k_hbm, v_hbm,
+    n_out, qg_out, kg_out, vg_out,
+    t_v, kl_v, vl_v, k_v, v_v, kg_v, vg_v, n_v, qg_v,
+    in_sem, out_sem, pass_sem,
+):
+    half = N // 2
+    loads = []
+    for p in range(2):
+        heads, wide = pl.ds(p * half, half), pl.ds(p * half * DH, half * DH)
+        pairs = (
+            (t_hbm.at[heads], t_v.at[heads]),
+            (v_hbm.at[:, wide], v_v.at[:, wide]),
+            (k_hbm.at[:, wide], k_v.at[:, wide]),
+            (kl_hbm.at[heads], kl_v.at[heads]),
+            (vl_hbm.at[heads], vl_v.at[heads]),
+        )
+        loads.append(
+            [pltpu.make_async_copy(a, b, in_sem.at[p, i]) for i, (a, b) in enumerate(pairs)]
+        )
+    passes = [
+        pltpu.make_async_copy(n_hbm, n_v, pass_sem.at[0]),
+        pltpu.make_async_copy(qg_hbm, qg_v, pass_sem.at[1]),
+    ]
+    for load in loads[0] + loads[1] + passes:
+        load.start()
+    stores = [
+        pltpu.make_async_copy(n_v, n_out, pass_sem.at[2]),
+        pltpu.make_async_copy(qg_v, qg_out, pass_sem.at[3]),
+    ]
+    for p in range(2):
+        for load in loads[p]:
+            load.wait()
+        for h in range(p * half, (p + 1) * half):
+            c = pl.ds(h * DH, DH)
+            kg_v[:, c] = (kl_v[h] + dot(v_v[:, c], t_v[h], 1, 1)).astype(BF16)
+            vg_v[:, c] = (vl_v[h] + dot(k_v[:, c], t_v[h], 1, 0)).astype(BF16)
+        wide = pl.ds(p * half * DH, half * DH)
+        for i, (src, dst) in enumerate(((kg_v, kg_out), (vg_v, vg_out))):
+            stores.append(
+                pltpu.make_async_copy(src.at[:, wide], dst.at[:, wide], out_sem.at[p, i])
+            )
+            stores[-1].start()
+        passes[p].wait()
+        stores[p].start()
     for store in stores:
         store.wait()
 
@@ -336,25 +364,42 @@
     eighths = pltpu.VMEM((2, MEMBERS, DH // MEMBERS, DH), F32)
     groups = pltpu.VMEM((2, GROUPS + 1, DH // MEMBERS, DH), F32)
     dma = pltpu.SemaphoreType.DMA
-    return pl.pallas_call(
+    whole = jax.ShapeDtypeStruct((tokens, width), BF16)
+    states = jax.ShapeDtypeStruct((N, DH, DH), BF16)
+    parts = jax.ShapeDtypeStruct((N, DH, DH), F32)
+    anywhere = pl.BlockSpec(memory_space=pl.ANY)
+    normed, query_grad, later, key_part, value_part = pl.pallas_call(
         kernel,
-        out_shape=[jax.ShapeDtypeStruct((tokens, width), BF16)] * 4,
-        in_specs=[pl.BlockSpec(memory_space=pl.ANY)] * 4,
-        out_specs=[pl.BlockSpec(memory_space=pl.ANY)] * 4,
+        out_shape=[whole, whole, states, parts, parts],
+        in_specs=[anywhere] * 4,
+        out_specs=[anywhere] * 5,
         scratch_shapes=[wide] * 4
-        + [blocks] * 10
+        + [blocks] * 9
         + [blocks] + [sums] * 4
-        + [wide] * 4
+        + [wide] * 2
         + [eighths, eighths, groups, eighths, eighths]
-        + [dma((4,)), dma((4,)), dma((2,)), dma((6,)), dma((6, N))]
+        + [dma((4,)), dma((4,)), dma((3,)), dma((6,)), dma((6, N))]
         + [dma((2, 3)), dma((2, MEMBERS)), dma((2, GROUPS)), dma((2, MEMBERS))],
         compiler_params=pltpu.CompilerParams(
             collective_id=0, has_side_effects=True, vmem_limit_bytes=60 * 1024 * 1024
         ),
         cost_estimate=pl.CostEstimate(
-            flops=2 * 14 * N * DH**3, bytes_accessed=16 * tokens * width, transcendentals=0
+            flops=2 * 12 * N * DH**3, bytes_accessed=16 * tokens * width, transcendentals=0
         ),
     )(q, k, v, g)
+    return pl.pallas_call(
+        finish,
+        out_shape=[whole] * 4,
+        in_specs=[anywhere] * 7,
+        out_specs=[anywhere] * 4,
+        scratch_shapes=[blocks, sums, sums]
+        + [wide] * 6
+        + [dma((2, 5)), dma((2, 2)), dma((4,))],
+        compiler_params=pltpu.CompilerParams(vmem_limit_bytes=60 * 1024 * 1024),
+        cost_estimate=pl.CostEstimate(
+            flops=2 * 2 * N * DH**3, bytes_accessed=18 * tokens * width, transcendentals=0
+        ),
+    )(normed, query_grad, later, key_part, value_part, k, v)
 
 
 def solution(mesh):

time: 83.1 us -> 74.8 us (0.900)
  local copies, waits for them, and re-layouts: 5.19 us -> 0 us
  Pallas kernels: 76.9 us -> 74 us
    unnamed x10 -> x0, local copies, waits for them, and re-layouts: 5.19 us -> none
    pallas_call x1 -> x2, Pallas kernels: 76.9 us -> 74 us  [the longest x1 70.4 us: shards(): pl.pallas_call(kernel, out_shape=[whole, whole, states, parts, parts], in...]
where the time goes in v2:
time: 74.8 us; the launch traced here: 74.7 us
  Pallas kernels  74 us (99%)
    pallas_call x1, Pallas kernels, shards(): pl.pallas_call(kernel, out_shape=[whole, whole, states, parts, parts], in...  70.4 us
    pallas_call x1, Pallas kernels, shards(): pl.pallas_call(finish, out_shape=[whole] * 4, in_specs=[anywhere] * 7, ou...  3.64 us

profile of v2, /device:TPU:1, one launch (start us, length us, event | category | flops | bytes accessed | tf_op | source)
XLA Modules:
  0.0 74.7 jit_solution(18408193263543579848)
XLA Ops:
  0.6 70.4 %shard_map.75 = (bf16[128,2048]{1,0:T(8,128)(2,1)}, bf16[128,2048]{1,0:T(8,128)(2,1)}, bf16[16,128,128]{2,1,0:T(8,128)(2,1)}, f32[16,128,128]{2,1,0:T(8,128)}, f32[16,128,128]{2,1,0:T(8,128)}) custom-call(bf16[128,2048]{1,0:T(8,128)(2,1)} %q_hbm.1, bf16[128,2048]{1,0:T(8,128)(2,1)} %k_hbm.3, bf16[128,2048]{1,0:T(8,128)(2,1)} %v_hbm.3, bf16[128,2048]{1,0:T(8,128)(2,1)} %g_hbm.1), custom_call_target="tpu_custom_call" | custom-call | flops 805306368 | bytes 4194304 | tf_op jit(solution)/shard_map/pallas_call | solution.py:371
  71.0 3.6 %shard_map.76 = (bf16[128,2048]{1,0:T(8,128)(2,1)}, bf16[128,2048]{1,0:T(8,128)(2,1)}, bf16[128,2048]{1,0:T(8,128)(2,1)}, bf16[128,2048]{1,0:T(8,128)(2,1)}) custom-call(bf16[128,2048]{1,0:T(8,128)(2,1)} %get-tuple-element.9.n_hbm, bf16[128,2048]{1,0:T(8,128)(2,1)} %get-tuple-element.10.qg_hbm, bf16[16,128,128]{2,1,0:T(8,128)(2,1)} %get-tuple-element.11.t_hbm, ...), custom_call_target="tpu_custom_call" | custom-call | flops 134217728 | bytes 4718592 | tf_op jit(solution)/shard_map/pallas_call | solution.py:390

commit v3 on v2

--- a/solution.py
+++ b/solution.py
@@ -7,6 +7,7 @@
 
 N = 16
 DH = 128
+PARTS = 2
 GROUPS = 4
 MEMBERS = 8
 EPS = 1e-06
@@ -14,7 +15,6 @@
     (2, 2), (2, 1), (1, 2), (2, 3), (3, 2), (1, 1), (3, 3), (1, 3), (3, 1),
     (2, 0), (0, 2), (1, 0), (0, 1), (3, 0), (0, 3),
 )
-EARLY = 0
 MESH = pl.DeviceIdType.MESH
 F32 = jnp.float32
 BF16 = jnp.bfloat16
@@ -33,7 +33,8 @@
     sc_v, al_v, sg_v, kl_v, vl_v,
     n_v, qg_v,
     za, zb, zc, zd, ze,
-    in_sem, out_sem, self_sem, send_sem, recv_sem, zsend_sem, z1_sem, z2_sem, z3_sem,
+    in_sem, out_sem, self_sem, send_sem, recv_sem,
+    zsend_sem, zacross_sem, z1_sem, z2_sem, z3_sem, ready_sem,
 ):
     me = lax.axis_index("head")
     seq = lax.axis_index("seq")
@@ -60,26 +61,32 @@
     y, x = me // 4, me % 4
     others = [lax.rem(y + dy, 4) * 4 + lax.rem(x + dx, 4) for dx, dy in STEPS]
 
+    def peers(reverse):
+        for j in range(1, GROUPS):
+            g = lax.rem(group + j, GROUPS)
+            yield (g, g < group, g > group) if reverse else (g, g > group, g < group)
+
     barrier = pltpu.get_barrier_semaphore()
     loads = [
         pltpu.make_async_copy(src, dst, in_sem.at[i])
         for i, (src, dst) in enumerate(((k_hbm, k_v), (v_hbm, v_v), (q_hbm, q_v), (g_hbm, g_v)))
     ]
-    for load in loads:
-        load.start()
-
-    @pl.loop(1, N)
-    def _(j):
-        pl.semaphore_signal(barrier, inc=1, device_id=plane(turn(j)), device_id_type=MESH)
+    loads[0].start()
+    loads[1].start()
+    for i in others:
+        pl.semaphore_signal(barrier, inc=1, device_id=plane(i), device_id_type=MESH)
+    for g, above, _ in peers(False):
+
+        @pl.when(above)
+        def _():
+            pl.semaphore_signal(barrier, inc=1, device_id=across(g), device_id_type=MESH)
 
     for j in range(1, MEMBERS):
         pl.semaphore_signal(
             barrier, inc=1, device_id=column(lax.rem(member + j, MEMBERS)), device_id_type=MESH
         )
-    for j in range(1, GROUPS):
-        pl.semaphore_signal(
-            barrier, inc=1, device_id=across(lax.rem(group + j, GROUPS)), device_id_type=MESH
-        )
+    loads[2].start()
+    loads[3].start()
 
     def send(which, src, dst, to):
         return pltpu.make_async_remote_copy(
@@ -113,7 +120,13 @@
         kv_s[h] = dot(k_v[:, cols(h)], v_v[:, cols(h)], 0, 0).astype(BF16)
 
     kv_r[me] = kv_s[me]
-    pl.semaphore_wait(barrier, N - 1 + MEMBERS - 1 + GROUPS - 1)
+    pl.semaphore_wait(barrier, N - 1 + MEMBERS - 1 + group)
+    for g, _, below in peers(False):
+
+        @pl.when(below)
+        def _():
+            pl.semaphore_signal(ready_sem.at[group], inc=1, device_id=across(g), device_id_type=MESH)
+
 
     for h in others:
         send(0, kv_s.at[h], kv_r.at[me], h).start()
@@ -140,9 +153,17 @@
         local = dot(scores, v_v[:, cols(h)], 1, 0)
         al_v[h] = local
         a_s[h] = local.astype(BF16)
-    for h in others:
-        send(3, a_s.at[h], a_r.at[me], h).start()
     a_r[me] = a_s[me]
+
+    def across_copy(z, g):
+        return pltpu.make_async_remote_copy(
+            src_ref=zc.at[z, GROUPS],
+            dst_ref=zc.at[z, group],
+            send_sem=zacross_sem.at[z, g],
+            recv_sem=z2_sem.at[z, group],
+            device_id=across(g),
+            device_id_type=MESH,
+        )
 
     def exchange(reverse, totals, first, second):
         z = 1 if reverse else 0
@@ -174,17 +195,28 @@
             total += zb[z, m]
         zc[z, GROUPS] = total
         zc[z, group] = jnp.zeros_like(total)
-        for j in range(1, GROUPS):
-            g = lax.rem(group + j, GROUPS)
-            zsend(1, zc.at[z, GROUPS], zc.at[z, group], z2_sem.at[z, group], across(g)).start()
+        for g, wanted, _ in peers(reverse):
+
+            @pl.when(wanted)
+            def _():
+                if not reverse:
+                    pl.semaphore_wait(ready_sem.at[g], 1)
+                across_copy(z, g).start()
+
         second()
-        for j in range(1, GROUPS):
-            g = lax.rem(group + j, GROUPS)
-            zwait(zc.at[z, g], z2_sem.at[z, g])
-        running = jnp.zeros_like(total)
-        for g in range(GROUPS):
-            counts = (g > group) if reverse else (g < group)
-            running += jnp.where(counts, zc[z, g], F32(0.0))
+        for g, _, given in peers(reverse):
+
+            @pl.when(given)
+            def _():
+                zwait(zc.at[z, g], z2_sem.at[z, g])
+
+            @pl.when(jnp.logical_not(given))
+            def _():
+                zc[z, g] = jnp.zeros_like(total)
+
+        running = zc[z, 0]
+        for g in range(1, GROUPS):
+            running += zc[z, g]
         for m in range(MEMBERS):
             m = MEMBERS - 1 - m if reverse else m
             zd[z, m] = running
@@ -202,9 +234,12 @@
         pltpu.make_async_copy(
             za.at[z, pl.ds(0, MEMBERS - 1)], za.at[z, pl.ds(0, MEMBERS - 1)], zsend_sem.at[z, 0]
         ).wait()
-        pltpu.make_async_copy(
-            zc.at[z, pl.ds(0, GROUPS - 1)], zc.at[z, pl.ds(0, GROUPS - 1)], zsend_sem.at[z, 1]
-        ).wait()
+        for g, wanted, _ in peers(z == 1):
+
+            @pl.when(wanted)
+            def _():
+                across_copy(z, g).wait_send()
+
         pltpu.make_async_copy(
             zd.at[z, pl.ds(0, MEMBERS - 1)], zd.at[z, pl.ds(0, MEMBERS - 1)], zsend_sem.at[z, 2]
         ).wait()
@@ -216,7 +251,11 @@
     total = kv_r[0].astype(F32)
     for i in range(1, N):
         total += kv_r[i].astype(F32)
-    state = exchange(False, total, lambda: None, lambda: None)
+    def send_rest():
+        for h in others:
+            send(3, a_s.at[h], a_r.at[me], h).start()
+
+    state = exchange(False, total, send_rest, lambda: None)
     for i in range(N):
         p_s[i] = state.astype(BF16)
         state += kv_r[i].astype(F32)
@@ -268,12 +307,21 @@
             kl_v[h] = dot(grads, q, 0, 0)
             vl_v[h] = dot(sc_v[h], out_grad, 0, 0)
 
+    stores = [
+        pltpu.make_async_copy(src, dst, out_sem.at[i])
+        for i, (src, dst) in enumerate(
+            ((n_v, n_hbm), (qg_v, qg_hbm), (kl_v, kl_hbm), (vl_v, vl_hbm))
+        )
+    ]
+
     def early():
         @pl.loop(1, N)
         def _(j):
             arrived(4, p_r, turn(j))
 
-        home(range(EARLY))
+        home(range(N))
+        for store in stores:
+            store.start()
 
     later = exchange(True, total, send_states, early)
     for i in range(N - 1, -1, -1):
@@ -283,16 +331,6 @@
         send(5, t_s.at[i], t_hbm.at[me], i).start()
     mine_t = pltpu.make_async_copy(t_s.at[me], t_hbm.at[me], self_sem.at[2])
     mine_t.start()
-    home(range(EARLY, N))
-
-    stores = [
-        pltpu.make_async_copy(src, dst, out_sem.at[i])
-        for i, (src, dst) in enumerate(
-            ((n_v, n_hbm), (qg_v, qg_hbm), (kl_v, kl_hbm), (vl_v, vl_hbm))
-        )
-    ]
-    for store in stores:
-        store.start()
 
     @pl.loop(1, N)
     def _(j):
@@ -313,9 +351,9 @@
     t_v, kl_v, vl_v, k_v, v_v, kg_v, vg_v, n_v, qg_v,
     in_sem, out_sem, pass_sem,
 ):
-    half = N // 2
+    half = N // PARTS
     loads = []
-    for p in range(2):
+    for p in range(PARTS):
         heads, wide = pl.ds(p * half, half), pl.ds(p * half * DH, half * DH)
         pairs = (
             (t_hbm.at[heads], t_v.at[heads]),
@@ -331,13 +369,13 @@
         pltpu.make_async_copy(n_hbm, n_v, pass_sem.at[0]),
         pltpu.make_async_copy(qg_hbm, qg_v, pass_sem.at[1]),
     ]
-    for load in loads[0] + loads[1] + passes:
+    for load in sum(loads, []) + passes:
         load.start()
     stores = [
         pltpu.make_async_copy(n_v, n_out, pass_sem.at[2]),
         pltpu.make_async_copy(qg_v, qg_out, pass_sem.at[3]),
     ]
-    for p in range(2):
+    for p in range(PARTS):
         for load in loads[p]:
             load.wait()
         for h in range(p * half, (p + 1) * half):
@@ -350,8 +388,9 @@
                 pltpu.make_async_copy(src.at[:, wide], dst.at[:, wide], out_sem.at[p, i])
             )
             stores[-1].start()
-        passes[p].wait()
-        stores[p].start()
+        if p < 2:
+            passes[p].wait()
+            stores[p].start()
     for store in stores:
         store.wait()
 
@@ -379,7 +418,8 @@
         + [wide] * 2
         + [eighths, eighths, groups, eighths, eighths]
         + [dma((4,)), dma((4,)), dma((3,)), dma((6,)), dma((6, N))]
-        + [dma((2, 3)), dma((2, MEMBERS)), dma((2, GROUPS)), dma((2, MEMBERS))],
+        + [dma((2, 3)), dma((2, GROUPS)), dma((2, MEMBERS)), dma((2, GROUPS)), dma((2, MEMBERS))]
+        + [pltpu.SemaphoreType.REGULAR((GROUPS,))],
         compiler_params=pltpu.CompilerParams(
             collective_id=0, has_side_effects=True, vmem_limit_bytes=60 * 1024 * 1024
         ),
@@ -394,7 +434,7 @@
         out_specs=[anywhere] * 4,
         scratch_shapes=[blocks, sums, sums]
         + [wide] * 6
-        + [dma((2, 5)), dma((2, 2)), dma((4,))],
+        + [dma((PARTS, 5)), dma((PARTS, 2)), dma((4,))],
         compiler_params=pltpu.CompilerParams(vmem_limit_bytes=60 * 1024 * 1024),
         cost_estimate=pl.CostEstimate(
             flops=2 * 2 * N * DH**3, bytes_accessed=18 * tokens * width, transcendentals=0

time: 74.8 us -> 70.3 us (0.940)
  Pallas kernels: 74 us -> 69.5 us
    pallas_call x1, Pallas kernels: 70.4 us -> 65.9 us  [shards(): pl.pallas_call(kernel, out_shape=[whole, whole, states, parts, parts], in...]
where the time goes in v3:
time: 70.3 us; the launch traced here: 70.2 us
  Pallas kernels  69.5 us (99%)
    pallas_call x1, Pallas kernels, shards(): pl.pallas_call(kernel, out_shape=[whole, whole, states, parts, parts], in...  65.9 us
    pallas_call x1, Pallas kernels, shards(): pl.pallas_call(finish, out_shape=[whole] * 4, in_specs=[anywhere] * 7, ou...  3.64 us

profile of v3, /device:TPU:1, one launch (start us, length us, event | category | flops | bytes accessed | tf_op | source)
XLA Modules:
  0.0 70.2 jit_solution(3687537866689028247)
XLA Ops:
  0.6 65.9 %shard_map.75 = (bf16[128,2048]{1,0:T(8,128)(2,1)}, bf16[128,2048]{1,0:T(8,128)(2,1)}, bf16[16,128,128]{2,1,0:T(8,128)(2,1)}, f32[16,128,128]{2,1,0:T(8,128)}, f32[16,128,128]{2,1,0:T(8,128)}) custom-call(bf16[128,2048]{1,0:T(8,128)(2,1)} %q_hbm.1, bf16[128,2048]{1,0:T(8,128)(2,1)} %k_hbm.3, bf16[128,2048]{1,0:T(8,128)(2,1)} %v_hbm.3, bf16[128,2048]{1,0:T(8,128)(2,1)} %g_hbm.1), custom_call_target="tpu_custom_call" | custom-call | flops 805306368 | bytes 4194304 | tf_op jit(solution)/shard_map/pallas_call | solution.py:410
  66.5 3.6 %shard_map.76 = (bf16[128,2048]{1,0:T(8,128)(2,1)}, bf16[128,2048]{1,0:T(8,128)(2,1)}, bf16[128,2048]{1,0:T(8,128)(2,1)}, bf16[128,2048]{1,0:T(8,128)(2,1)}) custom-call(bf16[128,2048]{1,0:T(8,128)(2,1)} %get-tuple-element.9.n_hbm, bf16[128,2048]{1,0:T(8,128)(2,1)} %get-tuple-element.10.qg_hbm, bf16[16,128,128]{2,1,0:T(8,128)(2,1)} %get-tuple-element.11.t_hbm, ...), custom_call_target="tpu_custom_call" | custom-call | flops 134217728 | bytes 4718592 | tf_op jit(solution)/shard_map/pallas_call | solution.py:430

commit v4 on v3

--- a/solution.py
+++ b/solution.py
@@ -8,8 +8,8 @@
 N = 16
 DH = 128
 PARTS = 2
-GROUPS = 4
-MEMBERS = 8
+GROUPS = 8
+MEMBERS = 4
 EPS = 1e-06
 STEPS = (
     (2, 2), (2, 1), (1, 2), (2, 3), (3, 2), (1, 1), (3, 3), (1, 3), (3, 1),
@@ -193,8 +193,8 @@
         total = zb[z, 0]
         for m in range(1, MEMBERS):
             total += zb[z, m]
-        zc[z, GROUPS] = total
-        zc[z, group] = jnp.zeros_like(total)
+        zc[z, GROUPS] = total.astype(BF16)
+        zc[z, group] = jnp.zeros(total.shape, BF16)
         for g, wanted, _ in peers(reverse):
 
             @pl.when(wanted)
@@ -212,11 +212,11 @@
 
             @pl.when(jnp.logical_not(given))
             def _():
-                zc[z, g] = jnp.zeros_like(total)
-
-        running = zc[z, 0]
+                zc[z, g] = jnp.zeros(total.shape, BF16)
+
+        running = zc[z, 0].astype(F32)
         for g in range(1, GROUPS):
-            running += zc[z, g]
+            running += zc[z, g].astype(F32)
         for m in range(MEMBERS):
             m = MEMBERS - 1 - m if reverse else m
             zd[z, m] = running
@@ -400,8 +400,8 @@
     wide = pltpu.VMEM((tokens, width), BF16)
     blocks = pltpu.VMEM((N, DH, DH), BF16)
     sums = pltpu.VMEM((N, DH, DH), F32)
-    eighths = pltpu.VMEM((2, MEMBERS, DH // MEMBERS, DH), F32)
-    groups = pltpu.VMEM((2, GROUPS + 1, DH // MEMBERS, DH), F32)
+    quarters = pltpu.VMEM((2, MEMBERS, DH // MEMBERS, DH), F32)
+    groups = pltpu.VMEM((2, GROUPS + 1, DH // MEMBERS, DH), BF16)
     dma = pltpu.SemaphoreType.DMA
     whole = jax.ShapeDtypeStruct((tokens, width), BF16)
     states = jax.ShapeDtypeStruct((N, DH, DH), BF16)
@@ -416,7 +416,7 @@
         + [blocks] * 9
         + [blocks] + [sums] * 4
         + [wide] * 2
-        + [eighths, eighths, groups, eighths, eighths]
+        + [quarters, quarters, groups, quarters, quarters]
         + [dma((4,)), dma((4,)), dma((3,)), dma((6,)), dma((6, N))]
         + [dma((2, 3)), dma((2, GROUPS)), dma((2, MEMBERS)), dma((2, GROUPS)), dma((2, MEMBERS))]
         + [pltpu.SemaphoreType.REGULAR((GROUPS,))],

time: 70.3 us -> 68.5 us (0.974)
  Pallas kernels: 69.5 us -> 67.7 us
    pallas_call x1, Pallas kernels: 65.9 us -> 64 us  [shards(): pl.pallas_call(kernel, out_shape=[whole, whole, states, parts, parts], in...]
where the time goes in v4:
time: 68.5 us; the launch traced here: 68.3 us
  Pallas kernels  67.7 us (99%)
    pallas_call x1, Pallas kernels, shards(): pl.pallas_call(kernel, out_shape=[whole, whole, states, parts, parts], in...  64 us
    pallas_call x1, Pallas kernels, shards(): pl.pallas_call(finish, out_shape=[whole] * 4, in_specs=[anywhere] * 7, ou...  3.64 us

profile of v4, /device:TPU:1, one launch (start us, length us, event | category | flops | bytes accessed | tf_op | source)
XLA Modules:
  0.0 68.3 jit_solution(7897442423171236124)
XLA Ops:
  0.6 64.0 %shard_map.75 = (bf16[128,2048]{1,0:T(8,128)(2,1)}, bf16[128,2048]{1,0:T(8,128)(2,1)}, bf16[16,128,128]{2,1,0:T(8,128)(2,1)}, f32[16,128,128]{2,1,0:T(8,128)}, f32[16,128,128]{2,1,0:T(8,128)}) custom-call(bf16[128,2048]{1,0:T(8,128)(2,1)} %q_hbm.1, bf16[128,2048]{1,0:T(8,128)(2,1)} %k_hbm.3, bf16[128,2048]{1,0:T(8,128)(2,1)} %v_hbm.3, bf16[128,2048]{1,0:T(8,128)(2,1)} %g_hbm.1), custom_call_target="tpu_custom_call" | custom-call | flops 805306368 | bytes 4194304 | tf_op jit(solution)/shard_map/pallas_call | solution.py:410
  64.7 3.6 %shard_map.76 = (bf16[128,2048]{1,0:T(8,128)(2,1)}, bf16[128,2048]{1,0:T(8,128)(2,1)}, bf16[128,2048]{1,0:T(8,128)(2,1)}, bf16[128,2048]{1,0:T(8,128)(2,1)}) custom-call(bf16[128,2048]{1,0:T(8,128)(2,1)} %get-tuple-element.9.n_hbm, bf16[128,2048]{1,0:T(8,128)(2,1)} %get-tuple-element.10.qg_hbm, bf16[16,128,128]{2,1,0:T(8,128)(2,1)} %get-tuple-element.11.t_hbm, ...), custom_call_target="tpu_custom_call" | custom-call | flops 134217728 | bytes 4718592 | tf_op jit(solution)/shard_map/pallas_call | solution.py:430

commit v5 on v4

--- a/solution.py
+++ b/solution.py
@@ -50,9 +50,6 @@
     def across(g):
         return (me, g * MEMBERS + member)
 
-    def turn(j):
-        return lax.rem(me + j, N)
-
     def cols(h):
         if isinstance(h, int):
             return pl.ds(h * DH, DH)
@@ -62,7 +59,7 @@
     others = [lax.rem(y + dy, 4) * 4 + lax.rem(x + dx, 4) for dx, dy in STEPS]
 
     def peers(reverse):
-        for j in range(1, GROUPS):
+        for j in (4, 3, 5, 2, 6, 1, 7):
             g = lax.rem(group + j, GROUPS)
             yield (g, g < group, g > group) if reverse else (g, g > group, g < group)
 
@@ -93,20 +90,15 @@
             src_ref=src,
             dst_ref=dst,
             send_sem=send_sem.at[which],
-            recv_sem=recv_sem.at[which, me],
+            recv_sem=recv_sem.at[which],
             device_id=plane(to),
             device_id_type=MESH,
         )
 
-    def arrived(which, buf, src):
-        pltpu.make_async_remote_copy(
-            src_ref=buf.at[src],
-            dst_ref=buf.at[src],
-            send_sem=send_sem.at[which],
-            recv_sem=recv_sem.at[which, src],
-            device_id=plane(me),
-            device_id_type=MESH,
-        ).wait_recv()
+    def arrived(which, buf):
+        pltpu.make_async_copy(
+            buf.at[pl.ds(0, N - 1)], buf.at[pl.ds(0, N - 1)], recv_sem.at[which]
+        ).wait()
 
     def all_sent(which, buf):
         pltpu.make_async_copy(
@@ -140,8 +132,6 @@
 
     for h in others:
         send(1, q_v.at[:, cols(h)], q_r.at[me], h).start()
-    for h in others:
-        send(2, g_v.at[:, cols(h)], g_r.at[me], h).start()
 
     rows = lax.broadcasted_iota(jnp.int32, (DH, DH), 0)
     causal = rows >= lax.broadcasted_iota(jnp.int32, (DH, DH), 1)
@@ -244,15 +234,15 @@
             zd.at[z, pl.ds(0, MEMBERS - 1)], zd.at[z, pl.ds(0, MEMBERS - 1)], zsend_sem.at[z, 2]
         ).wait()
 
-    @pl.loop(1, N)
-    def _(j):
-        arrived(0, kv_r, turn(j))
+    arrived(0, kv_r)
 
     total = kv_r[0].astype(F32)
     for i in range(1, N):
         total += kv_r[i].astype(F32)
     def send_rest():
         for h in others:
+            send(2, g_v.at[:, cols(h)], g_r.at[me], h).start()
+        for h in others:
             send(3, a_s.at[h], a_r.at[me], h).start()
 
     state = exchange(False, total, send_rest, lambda: None)
@@ -264,12 +254,9 @@
     mine_q.wait()
     mine_g.wait()
 
-    @pl.loop(1, N)
-    def _(j):
-        i = turn(j)
-        arrived(1, q_r, i)
-        arrived(2, g_r, i)
-        arrived(3, a_r, i)
+    arrived(1, q_r)
+    arrived(2, g_r)
+    arrived(3, a_r)
 
     def normalize(attn, cot):
         inv_rms = lax.rsqrt(jnp.mean(attn * attn, axis=-1, keepdims=True) + EPS)
@@ -315,26 +302,26 @@
     ]
 
     def early():
-        @pl.loop(1, N)
-        def _(j):
-            arrived(4, p_r, turn(j))
+        after = jnp.zeros((DH, DH), F32)
+        for i in range(N - 1, -1, -1):
+            mine = sg_v[i]
+            sg_v[i] = after
+            after += mine
+        arrived(4, p_r)
 
         home(range(N))
         for store in stores:
             store.start()
 
     later = exchange(True, total, send_states, early)
-    for i in range(N - 1, -1, -1):
-        t_s[i] = later.astype(BF16)
-        later += sg_v[i]
     for i in others:
+        t_s[i] = (sg_v[i] + later).astype(BF16)
         send(5, t_s.at[i], t_hbm.at[me], i).start()
+    t_s[me] = (sg_v[me] + later).astype(BF16)
     mine_t = pltpu.make_async_copy(t_s.at[me], t_hbm.at[me], self_sem.at[2])
     mine_t.start()
 
-    @pl.loop(1, N)
-    def _(j):
-        arrived(5, t_hbm, turn(j))
+    arrived(5, t_hbm)
 
     mine_t.wait()
     for which, buf in enumerate((kv_s, q_r, g_r, a_s, p_s, t_s)):
@@ -417,7 +404,7 @@
         + [blocks] + [sums] * 4
         + [wide] * 2
         + [quarters, quarters, groups, quarters, quarters]
-        + [dma((4,)), dma((4,)), dma((3,)), dma((6,)), dma((6, N))]
+        + [dma((4,)), dma((4,)), dma((3,)), dma((6,)), dma((6,))]
         + [dma((2, 3)), dma((2, GROUPS)), dma((2, MEMBERS)), dma((2, GROUPS)), dma((2, MEMBERS))]
         + [pltpu.SemaphoreType.REGULAR((GROUPS,))],
         compiler_params=pltpu.CompilerParams(

time: 68.5 us -> 67.6 us (0.987)
  Pallas kernels: 67.7 us -> 66.8 us
    pallas_call x1, Pallas kernels: 64 us -> 63.1 us  [shards(): pl.pallas_call(kernel, out_shape=[whole, whole, states, parts, parts], in...]
where the time goes in v5:
time: 67.6 us; the launch traced here: 67.4 us
  Pallas kernels  66.8 us (99%)
    pallas_call x1, Pallas kernels, shards(): pl.pallas_call(kernel, out_shape=[whole, whole, states, parts, parts], in...  63.1 us
    pallas_call x1, Pallas kernels, shards(): pl.pallas_call(finish, out_shape=[whole] * 4, in_specs=[anywhere] * 7, ou...  3.64 us

profile of v5, /device:TPU:1, one launch (start us, length us, event | category | flops | bytes accessed | tf_op | source)
XLA Modules:
  0.0 67.4 jit_solution(13981330031772759040)
XLA Ops:
  0.6 63.1 %shard_map.75 = (bf16[128,2048]{1,0:T(8,128)(2,1)}, bf16[128,2048]{1,0:T(8,128)(2,1)}, bf16[16,128,128]{2,1,0:T(8,128)(2,1)}, f32[16,128,128]{2,1,0:T(8,128)}, f32[16,128,128]{2,1,0:T(8,128)}) custom-call(bf16[128,2048]{1,0:T(8,128)(2,1)} %q_hbm.1, bf16[128,2048]{1,0:T(8,128)(2,1)} %k_hbm.3, bf16[128,2048]{1,0:T(8,128)(2,1)} %v_hbm.3, bf16[128,2048]{1,0:T(8,128)(2,1)} %g_hbm.1), custom_call_target="tpu_custom_call" | custom-call | flops 805306368 | bytes 4194304 | tf_op jit(solution)/shard_map/pallas_call | solution.py:397
  63.8 3.6 %shard_map.76 = (bf16[128,2048]{1,0:T(8,128)(2,1)}, bf16[128,2048]{1,0:T(8,128)(2,1)}, bf16[128,2048]{1,0:T(8,128)(2,1)}, bf16[128,2048]{1,0:T(8,128)(2,1)}) custom-call(bf16[128,2048]{1,0:T(8,128)(2,1)} %get-tuple-element.9.n_hbm, bf16[128,2048]{1,0:T(8,128)(2,1)} %get-tuple-element.10.qg_hbm, bf16[16,128,128]{2,1,0:T(8,128)(2,1)} %get-tuple-element.11.t_hbm, ...), custom_call_target="tpu_custom_call" | custom-call | flops 134217728 | bytes 4718592 | tf_op jit(solution)/shard_map/pallas_call | solution.py:417
